TPU v7x, 256 devices: a whole 4x4x8 slice. The times are simulated.
256 devices in a mesh: dp: 16 (over z, x_lo), ctx: 16 (over x_hi, y, core).
Axes of the slice: x: 4 (x_hi: 2, x_lo: 2; x = x_hi * 2 + x_lo), y: 4, z: 8, core: 2. Of those that a mesh axis runs over, the one named last changes fastest.
Arguments:
- hidden: bfloat16 [16, 2048, 4096], P('dp', 'ctx'), may hold values from -6 to 6
- queries: bfloat16 [16, 2048, 4096], P('dp', 'ctx'), may hold values from -5 to 5
- keys: bfloat16 [16, 2048, 512], P('dp', 'ctx'), may hold values from -5 to 5
- values: bfloat16 [16, 2048, 512], P('dp', 'ctx'), may hold values from -8 to 8
- upstream: bfloat16 [16, 2048, 4096], P('dp', 'ctx'), may hold values from -0.19824219 to 0.19824219
Outputs:
- attended: bfloat16 [16, 2048, 4096], P('dp', 'ctx')
- kv_grads: float32 [4096, 1024], P(('dp', 'ctx'))
All inputs are finite; a program needn't handle non-finite values.
Results may differ from a plain program's by a relative error of at most 0.015.
Values may be sent and summed in bfloat16 or wider, within the bound.
A program may use at most 128 MiB of HBM per device.

v0:
```python
import jax
import jax.numpy as jnp
from jax import lax
from jax.sharding import PartitionSpec as P

H = 32
KV = 4
HD = 128


def attend(query_local, key_local, value_local, grad_local):
    length = query_local.shape[0]
    kv_local = key_local.shape[1] // HD
    group_size = query_local.shape[1] // HD // kv_local
    inv_root = HD ** (-0.5)
    block_rows = 512
    keys3 = key_local.reshape(length, kv_local, HD)
    vals3 = value_local.reshape(length, kv_local, HD)
    positions = jnp.arange(length)

    def block_step(running, first_row):
        key_acc, val_acc = running
        query_block = lax.dynamic_slice_in_dim(query_local, first_row, block_rows, 0)
        query_block = query_block.reshape(block_rows, kv_local, group_size, HD)
        grad_block = lax.dynamic_slice_in_dim(grad_local, first_row, block_rows, 0)
        grad_block = grad_block.reshape(block_rows, kv_local, group_size, HD)
        scores = (
            jnp.einsum("qgrd,kgd->grqk", query_block, keys3, preferred_element_type=jnp.float32)
            * inv_root
        )
        rows_at = first_row + jnp.arange(block_rows)
        allowed = positions[None, :] <= rows_at[:, None]
        scores = jnp.where(allowed, scores, -jnp.inf)
        chances = jnp.exp(scores - jnp.max(scores, axis=-1, keepdims=True))
        chances = chances / jnp.sum(chances, axis=-1, keepdims=True)
        shares = chances.astype(jnp.bfloat16)
        attended = jnp.einsum(
            "grqk,kgd->qgrd", shares, vals3, preferred_element_type=jnp.float32
        ).astype(jnp.bfloat16)
        dshares = jnp.einsum(
            "qgrd,kgd->grqk", grad_block, vals3, preferred_element_type=jnp.float32
        )
        inner_sum = jnp.sum(chances * dshares, axis=-1, keepdims=True)
        dscores = (chances * (dshares - inner_sum) * inv_root).astype(jnp.bfloat16)
        key_acc = key_acc + jnp.einsum(
            "grqk,qgrd->kgrd", dscores, query_block, preferred_element_type=jnp.float32
        )
        val_acc = val_acc + jnp.einsum(
            "grqk,qgrd->kgrd", shares, grad_block, preferred_element_type=jnp.float32
        )
        return ((key_acc, val_acc), attended.reshape(block_rows, kv_local * group_size * HD))

    empty_acc = jnp.zeros((length, kv_local, group_size, HD), jnp.float32)
    starts = jnp.arange(length // block_rows, dtype=jnp.int32) * block_rows
    (key_acc, val_acc), blocks = lax.scan(block_step, (empty_acc, empty_acc), starts)
    attended = blocks.reshape(length, kv_local * group_size * HD)
    key_terms = key_acc.astype(jnp.bfloat16).reshape(length, kv_local * group_size * HD)
    value_terms = val_acc.astype(jnp.bfloat16).reshape(length, kv_local * group_size * HD)
    return (attended, key_terms, value_terms)


def group_total(terms, seq_rows):
    summed = terms.astype(jnp.float32).reshape(seq_rows, KV, H // KV, HD).sum(axis=2)
    return summed.astype(jnp.bfloat16).reshape(seq_rows, KV * HD)


def per_device(hidden, queries, keys, values, upstream):
    query_rows = queries[0]
    grad_rows = upstream[0]
    seq_rows = query_rows.shape[0]
    keys3 = keys[0].reshape(seq_rows, KV, HD)
    vals3 = values[0].reshape(seq_rows, KV, HD)
    key_send = jnp.repeat(keys3, H // KV, axis=1).reshape(seq_rows, H * HD)
    value_send = jnp.repeat(vals3, H // KV, axis=1).reshape(seq_rows, H * HD)
    query_local, key_local, value_local, grad_local = (
        lax.all_to_all(query_rows, "ctx", split_axis=1, concat_axis=0, tiled=True),
        lax.all_to_all(key_send, "ctx", split_axis=1, concat_axis=0, tiled=True),
        lax.all_to_all(value_send, "ctx", split_axis=1, concat_axis=0, tiled=True),
        lax.all_to_all(grad_rows, "ctx", split_axis=1, concat_axis=0, tiled=True),
    )
    attended, key_terms, value_terms = attend(query_local, key_local, value_local, grad_local)
    attended_rows, key_back, value_back = (
        lax.all_to_all(attended, "ctx", split_axis=0, concat_axis=1, tiled=True),
        lax.all_to_all(key_terms, "ctx", split_axis=0, concat_axis=1, tiled=True),
        lax.all_to_all(value_terms, "ctx", split_axis=0, concat_axis=1, tiled=True),
    )
    key_grads = group_total(key_back, seq_rows)
    value_grads = group_total(value_back, seq_rows)
    kv_rows = jnp.concatenate([key_grads, value_grads], axis=1)
    hidden_rows = hidden[0]
    share = lax.psum_scatter(
        lax.dot_general(
            hidden_rows, kv_rows, (((0,), (0,)), ((), ())), preferred_element_type=jnp.float32
        ),
        ("dp", "ctx"),
        scatter_dimension=0,
        tiled=True,
    )
    return (attended_rows[None], share)


def solution(mesh):
    return jax.shard_map(
        per_device,
        mesh=mesh,
        in_specs=(
            P("dp", "ctx", None),
            P("dp", "ctx", None),
            P("dp", "ctx", None),
            P("dp", "ctx", None),
            P("dp", "ctx", None),
        ),
        out_specs=(P("dp", "ctx", None), P(("dp", "ctx"), None)),
        check_vma=False,
    )
```

profile of v0, /device:TPU:1, one launch (start us, length us, event | category | flops | bytes accessed | tf_op | source)
XLA Modules:
  0.0 1600.8 jit_solution(864994109973320216)
XLA Ops:
  9.5 8.4 all-to-all-start.3
  19.0 16.2 %all-to-all-done.3 = bf16[128,16,256]{0,2,1:T(8,128)(2,1)S(1)} async-done(((bf16[128,16,256]{0,2,1:T(8,128)(2,1)}), bf16[128,16,256]{0,2,1:T(8,128)(2,1)S(1)}, u32[]{:S(2)}, u32[]{:S(2)}) %all-to-all-start.3) | async-done | bytes 1048608 | tf_op jit(solution)/shard_map/all_to_all | solution.py:78
  36.4 4.4 all-to-all-start.1
  43.0 15.0 all-to-all-done.1
  58.0 5.0 all-to-all-start
  65.3 15.1 all-to-all-done
  80.4 5.0 all-to-all-start.2
  94.2 8.6 all-to-all-done.2
  105.1 127.7 %while.15 = (s32[]{:T(128)}, f32[2048,2,1,128]{0,3,1,2:T(8,128)}, f32[2048,2,1,128]{0,3,1,2:T(8,128)}, bf16[4,512,256]{2,1,0:T(8,128)(2,1)}, s32[4]{0:T(128)S(1)...) while((s32[]{:T(128)}, f32[2048,2,1,128]{0,3,1,2:T(8,128)}, ...), condition=%wide.region_4.5_spmd.clone, body=%wide.region_0.4_spmd.clone.sunk | while | flops 2752640512 | bytes 174383504 | solution.py:55
  119.9 7.4 fusion.81
  127.3 3.6 fusion.79
  130.9 4.2 fusion.80
  141.8 3.4 fusion.77
  151.4 8.0 fusion.81
  159.4 3.6 fusion.79
  163.0 4.2 fusion.80
  173.9 3.4 fusion.77
  183.4 8.0 fusion.81
  191.5 3.6 fusion.79
  195.1 4.2 fusion.80
  206.0 3.4 fusion.77
  215.5 8.0 fusion.81
  223.6 3.6 fusion.79
  227.2 4.2 fusion.80
  236.0 4.4 all-to-all-start.5
  243.6 14.0 all-to-all-done.5
  257.6 4.4 all-to-all-start.6
  262.2 17.1 %all-to-all-done.6 = bf16[16,128,256]{1,2,0:T(8,128)(2,1)S(1)} async-done(((bf16[16,128,256]{1,2,0:T(8,128)(2,1)}), bf16[16,128,256]{1,2,0:T(8,128)(2,1)S(1)}, u32[]{:S(2)}, u32[]{:S(2)}) %all-to-all-start.6) | async-done | bytes 1048608 | tf_op jit(solution)/shard_map/all_to_all | solution.py:85
  279.4 8.1 convolution_bitcast_fusion
  287.5 17.4 %copy.79 = f32[4096,1024]{1,0:T(8,128)} copy(f32[4096,1024]{0,1:T(8,128)} %convolution_bitcast_fusion) | data formatting | bytes 33554432
  306.2 21.0 %all_to_all.112 = bf16[16,128,256]{2,1,0:T(8,128)(2,1)S(1)} all-to-all(bf16[16,128,256]{2,1,0:T(8,128)(2,1)S(1)} %bitcast.209), channel_id=1, replica_groups=mesh['dp'=16,'ctx'=16] {'ctx'}, dimensions={0} | all-to-all | bytes 2097152 | tf_op jit(solution)/shard_map/all_to_all | solution.py:83
  329.2 1264.7 %reduce-scatter.4.cloned.1.call-done = f32[16,1024]{1,0:T(8,128)} async-done(((f32[4096,1024]{1,0:T(8,128)}), f32[16,1024]{1,0:T(8,128)}) %reduce-scatter.4.cloned.1.call-update) | async-done | bytes 65552
  (134 shorter events, 76.9 us)
Async XLA Ops:
  7.2 272.3 %copy-start = (bf16[1,128,4096]{2,1,0:T(8,128)(2,1)S(1)}, bf16[1,128,4096]{2,1,0:T(8,128)(2,1)}, u32[]{:S(2)}) copy-start(bf16[1,128,4096]{2,1,0:T(8,128)(2,1)} %param.7) | copy-start | bytes 3145732
  9.5 25.7 %all-to-all-start.3 = ((bf16[128,16,256]{0,2,1:T(8,128)(2,1)}), bf16[128,16,256]{0,2,1:T(8,128)(2,1)S(1)}, u32[]{:S(2)}, u32[]{:S(2)}) async-start(bf16[128,16,256]{0,2,1:T(8,128)(2,1)} %bitcast.10), calls=%async_computation.3 | async-start | bytes 2097152 | tf_op jit(solution)/shard_map/all_to_all | solution.py:78
  36.4 21.6 %all-to-all-start.1 = ((bf16[128,16,256]{0,2,1:T(8,128)(2,1)}), bf16[128,16,256]{0,2,1:T(8,128)(2,1)S(1)}, u32[]{:S(2)}, u32[]{:S(2)}) async-start(bf16[128,16,256]{0,2,1:T(8,128)(2,1)} %bitcast.204), calls=%async_computation.1 | async-start | bytes 2097152 | tf_op jit(solution)/shard_map/all_to_all | solution.py:77
  58.0 22.4 %all-to-all-start = ((bf16[128,16,256]{0,2,1:T(8,128)(2,1)}), bf16[128,16,256]{0,2,1:T(8,128)(2,1)}, u32[]{:S(2)}, u32[]{:S(2)}) async-start(bf16[128,16,256]{0,2,1:T(8,128)(2,1)} %bitcast.203), calls=%async_computation | async-start | bytes 2097152 | tf_op jit(solution)/shard_map/all_to_all | solution.py:76
  80.4 22.4 %all-to-all-start.2 = ((bf16[128,16,256]{0,2,1:T(8,128)(2,1)}), bf16[128,16,256]{0,2,1:T(8,128)(2,1)}, u32[]{:S(2)}, u32[]{:S(2)}) async-start(bf16[128,16,256]{0,2,1:T(8,128)(2,1)} %bitcast.200), calls=%async_computation.2 | async-start | bytes 2097152 | tf_op jit(solution)/shard_map/all_to_all | solution.py:79
  110.4 5.9 copy-start.4
  113.8 5.3 copy-start.1
  119.2 8.1 slice-start
  119.9 7.4 slice-start.1
  119.9 7.4 copy-start.5
  127.3 3.6 copy-start.2
  141.8 5.9 copy-start.4
  145.2 5.3 copy-start.1
  150.6 8.8 slice-start
  151.4 8.0 slice-start.1
  151.4 8.0 copy-start.5
  159.4 3.6 copy-start.2
  173.9 5.9 copy-start.4
  177.3 5.3 copy-start.1
  182.7 8.8 slice-start
  183.4 8.0 slice-start.1
  183.4 8.0 copy-start.5
  191.5 3.6 copy-start.2
  206.0 5.9 copy-start.4
  209.4 5.3 copy-start.1
  214.8 8.8 slice-start
  215.5 8.0 slice-start.1
  215.5 8.0 copy-start.5
  223.6 3.6 copy-start.2
  236.0 21.6 %all-to-all-start.5 = ((bf16[16,128,256]{1,2,0:T(8,128)(2,1)}), bf16[16,128,256]{1,2,0:T(8,128)(2,1)S(1)}, u32[]{:S(2)}, u32[]{:S(2)}) async-start(bf16[16,128,256]{1,2,0:T(8,128)(2,1)} %copy.70), calls=%async_computation.5 | async-start | bytes 2097152 | tf_op jit(solution)/shard_map/all_to_all | solution.py:84
  257.6 21.6 %all-to-all-start.6 = ((bf16[16,128,256]{1,2,0:T(8,128)(2,1)}), bf16[16,128,256]{1,2,0:T(8,128)(2,1)S(1)}, u32[]{:S(2)}, u32[]{:S(2)}) async-start(bf16[16,128,256]{1,2,0:T(8,128)(2,1)} %copy.71), calls=%async_computation.6 | async-start | bytes 2097152 | tf_op jit(solution)/shard_map/all_to_all | solution.py:85
  262.0 1332.0 %reduce-scatter.4.cloned.1.call-start = ((), (), s32[]{:S(2)}) async-start(), calls=%async_computation.8 | async-start | bytes 16842752
  (5 other events, 6.7 us)
Sparse Core Ops, SparseCore 0:
  305.1 1288.8 reduce-scatter.3
where the time goes:
time: 1610 us; the launch traced here: 1600 us
  waiting for transfers between devices  1350 us (84%)
  matrix products  95.1 us (6%)
  local copies, waits for them, and re-layouts  60.9 us (4%)
  starting transfers between devices  31.5 us (2%)
  blocking collectives  21 us (1%)
  other arithmetic  19.1 us (1%)
    unnamed x2, waiting for transfers between devices  1260 us
  transfers between devices with their start and end apart: 7, of which 7 were waited for; matrix products, arithmetic and copies ran while one was open for 1% of the time, Pallas kernels for 0%

commit v1 on v0

v1 whole, which is shorter than its diff:
```python
import math

import jax
import jax.numpy as jnp
from jax import lax
from jax.experimental import pallas as pl
from jax.experimental.pallas import tpu as pltpu
from jax.sharding import PartitionSpec as P

MESH = pl.DeviceIdType.MESH
HD = 128
L = 2048
ROWS = 128
B = 512
NB = L // B
G2 = 2 * HD
D = 4096
EXP_SCALE = (HD**-0.5) * math.log2(math.e)
NEG = -1e30
f32 = jnp.float32
bf16 = jnp.bfloat16

CHIPS = [(1, 2), (0, 1), (1, 1), (0, 3), (1, 3), (0, 2), (1, 0)]


def dot(a, b):
    return lax.dot_general(a, b, (((1,), (0,)), ((), ())), preferred_element_type=f32)


def col_max(s):
    return jnp.max(s.reshape(s.shape[0] // 8, 8, s.shape[1]), axis=0)


def col_sum(s):
    return jnp.sum(s.reshape(s.shape[0] // 8, 8, s.shape[1]), axis=0)


def rows_of(i, n=B):
    return pl.ds(pl.multiple_of(i * n, n), n)


def pair_index(i, j):
    return i * (i + 1) // 2 + j


def kernel(
    hid_in, q_in, k_in, v_in, g_in, att_out, grad_out,
    q_buf, g_buf, kv_buf, hid_v, ht_src, h_buf, att_buf, vt, qt_scr, s_scr, p_scr, ot_scr, li_scr,
    gt_scr, gs_scr, dd_scr, own, s1_src, s1_dst, s1_sum, s2_src, s2_dst, kv_all, acc, rs_src, rs_dst,
    q_ss, q_rs, g_ss, g_rs, kv_ss, kv_rs, sib_ss, sib_rs, h_ss, h_rs, att_ss, att_rs, hid_sem,
    s1_ss, s1_rs, s2_ss, s2_rs, s3_ss, s3_rs, s4_ss, s4_rs, rs_ss, rs_rs,
):
    dp = lax.axis_index("dp")
    me = lax.axis_index("ctx")
    xh, y, core = me // 8, (me // 2) % 4, me % 2
    sib = me + 1 - 2 * core
    group = me // 4
    half = y % 2

    def at(dx, dy, c):
        return ((xh + dx) % 2) * 8 + ((y + dy) % 4) * 2 + c

    def remote(src, dst, ss, rs, c=None, d=None):
        return pltpu.make_async_remote_copy(
            src_ref=src, dst_ref=dst, send_sem=ss, recv_sem=rs,
            device_id=(dp if d is None else d, me if c is None else c), device_id_type=MESH,
        )

    barrier = pltpu.get_barrier_semaphore()

    def greet(i, _):
        pl.semaphore_signal(barrier, inc=1, device_id=(dp, (me + i) % 16), device_id_type=MESH)
        pl.semaphore_signal(barrier, inc=1, device_id=((dp + i) % 16, me), device_id_type=MESH)
        return 0

    lax.fori_loop(1, 16, greet, 0)
    hid_copy = pltpu.make_async_copy(hid_in.at[0], hid_v, hid_sem)
    hid_copy.start()
    pl.semaphore_wait(barrier, 30)

    my_rows = rows_of(me, ROWS)

    def kv_copy(c, which):
        src = (k_in, v_in)[which].at[0, :, pl.ds(pl.multiple_of((c // 4) * HD, HD), HD)]
        return src, kv_buf.at[which, my_rows]

    def kv_send(c, which):
        src, dst = kv_copy(c, which)
        remote(src, dst, kv_ss.at[c], kv_rs.at[me], c=c).start()

    def kv_keep(which):
        src, dst = kv_copy(me, which)
        pltpu.make_async_copy(src, dst, kv_rs.at[me]).start()

    def head_cols(c):
        return pl.ds(pl.multiple_of(c * G2, G2), G2)

    def q_copy(c):
        return remote(q_in.at[0, :, head_cols(c)], q_buf.at[my_rows], q_ss.at[c], q_rs.at[me], c=c)

    def g_copy(c):
        return remote(g_in.at[0, :, head_cols(c)], g_buf.at[my_rows], g_ss.at[c], g_rs.at[me], c=c)

    def h_dst():
        return h_buf.at[:, :, my_rows]

    def h_copy(c):
        return remote(ht_src.at[:, c], h_dst(), h_ss.at[c], h_rs.at[me], c=c)

    peers = [at(dx, dy, c) for c in (0, 1) for dx, dy in CHIPS]
    for c, which in zip(peers, [0] * 7 + [1] * 7, strict=True):
        kv_send(c, which)

    @pl.when(core == 0)
    def _():
        kv_keep(0)
        kv_send(sib, 1)

    @pl.when(core == 1)
    def _():
        kv_keep(1)
        kv_send(sib, 0)

    peers = [at(dx, dy, (core + c) % 2) for c in (0, 1) for dx, dy in CHIPS] + [sib]
    for c in peers:
        q_copy(c).start()
    pltpu.make_async_copy(q_in.at[0, :, head_cols(me)], q_buf.at[my_rows], q_rs.at[me]).start()
    for c in peers:
        g_copy(c).start()
    pltpu.make_async_copy(g_in.at[0, :, head_cols(me)], g_buf.at[my_rows], g_rs.at[me]).start()

    hid_copy.wait()

    def turn(b, _):
        ht_src[b] = hid_v[:, pl.ds(pl.multiple_of(b * 256, 256), 256)].T.reshape(16, 16, ROWS)
        return 0

    lax.fori_loop(0, 16, turn, 0)
    for c in peers:
        h_copy(c).start()
    pltpu.make_async_copy(ht_src.at[:, me], h_dst(), h_rs.at[me]).start()

    def kv_wait(s, _):
        part = kv_buf.at[core, rows_of(s, ROWS)]
        pltpu.make_async_copy(part, part, kv_rs.at[s]).wait()
        return 0

    lax.fori_loop(0, 16, kv_wait, 0)
    sib_copy = remote(kv_buf.at[core], kv_buf.at[core], sib_ss, sib_rs, c=sib)
    sib_copy.start()
    theirs = kv_buf.at[1 - core]
    pltpu.make_async_copy(theirs, theirs, sib_rs).wait()

    def turn_v(j, _):
        vt[j] = kv_buf[1, rows_of(j), :].T
        return 0

    lax.fori_loop(0, NB, turn_v, 0)

    def wait_rows(buf, sems, i):
        def one(s, _):
            part = buf.at[rows_of(s, ROWS)]
            pltpu.make_async_copy(part, part, sems.at[s]).wait()
            return 0

        lax.fori_loop(4 * i, 4 * i + 4, one, 0)

    def q_turned(i):
        r = rows_of(i)
        return jnp.concatenate([q_buf[r, 0:HD].T, q_buf[r, HD:G2].T], axis=1)

    def k_block(j):
        return kv_buf[0, rows_of(j), :]

    def causal(s):
        key_at = lax.broadcasted_iota(jnp.int32, (B, 2 * B), 0)
        query_at = lax.broadcasted_iota(jnp.int32, (B, 2 * B), 1) % B
        return jnp.where(key_at <= query_at, s, NEG)

    def att_copy(s):
        return remote(
            att_buf.at[rows_of(s, ROWS)], att_out.at[0, :, head_cols(me)], att_ss.at[s], att_rs.at[me], c=s
        )

    def att_send(s, _):
        @pl.when(s != me)
        def _():
            att_copy(s).start()

        @pl.when(s == me)
        def _():
            pltpu.make_async_copy(att_buf.at[my_rows], att_out.at[0, :, head_cols(me)], att_rs.at[me]).start()

        return 0

    wait_rows(q_buf, q_rs, 0)
    first = causal(dot(k_block(0), q_turned(0)))
    s_scr[0, 0] = first

    def forward(i, top):
        now, later = i % 2, 1 - i % 2
        shift = jnp.max(top, axis=0, keepdims=True) * EXP_SCALE
        nxt = jnp.minimum(i + 1, NB - 1)

        @pl.when(i + 1 < NB)
        def _():
            wait_rows(q_buf, q_rs, i + 1)

        qt_scr[...] = q_turned(nxt)

        def weigh(j, carry):
            l, o, mn = carry
            e = jnp.exp2(s_scr[now, j] * EXP_SCALE - shift)
            l = l + col_sum(e)
            eb = e.astype(bf16)
            p_scr[pair_index(i, j)] = eb
            return l, o + dot(vt[j], eb), mn

        def step(j, carry):
            l, o, mn = carry
            s = dot(k_block(j), qt_scr[...])
            s_scr[later, j] = s
            return weigh(j, (l, o, jnp.maximum(mn, col_max(s))))

        start = (jnp.zeros((8, 2 * B), f32), jnp.zeros((HD, 2 * B), f32), jnp.full((8, 2 * B), NEG, f32))
        carry = lax.fori_loop(0, i, step, start)
        l, o, mn = lax.cond(nxt > i, lambda c: step(i, c), lambda c: weigh(i, c), carry)
        s = causal(dot(k_block(nxt), qt_scr[...]))
        s_scr[later, nxt] = s
        mn = jnp.maximum(mn, col_max(s))
        li = 1.0 / jnp.sum(l, axis=0, keepdims=True)
        o = o * li
        ot_scr[i] = o
        li_scr[i] = jnp.broadcast_to(li, (8, 2 * B))
        r = rows_of(i)
        att_buf[r, 0:HD] = o[:, 0:B].T.astype(bf16)
        att_buf[r, HD:G2] = o[:, B : 2 * B].T.astype(bf16)
        lax.fori_loop(4 * i, 4 * i + 4, att_send, 0)
        return mn

    lax.fori_loop(0, NB, forward, col_max(first))

    def prepare(i, _):
        wait_rows(g_buf, g_rs, i)
        r = rows_of(i)
        gt = jnp.concatenate([g_buf[r, 0:HD].T, g_buf[r, HD:G2].T], axis=1).astype(f32)
        gs = (gt * li_scr[i][0:1, :]).astype(bf16)
        gt_scr[i] = gs
        gs_scr[i] = gs.T
        dd = jnp.sum(gs.astype(f32) * ot_scr[i], axis=0, keepdims=True)
        dd_scr[i] = jnp.broadcast_to(dd, (8, 2 * B))
        return 0

    lax.fori_loop(0, NB, prepare, 0)

    def backward(j):
        vj = kv_buf[1, rows_of(j), :]

        def step(i, carry):
            dk, dv = carry
            eb = p_scr[pair_index(i, j)]
            dpr = dot(vj, gt_scr[i])
            ds = (eb.astype(f32) * (dpr - dd_scr[i][0:1, :])).astype(bf16)
            r = rows_of(i)
            qc = jnp.concatenate([q_buf[r, 0:HD], q_buf[r, HD:G2]], axis=0)
            return dk + dot(ds, qc), dv + dot(eb, gs_scr[i])

        zero = jnp.zeros((B, HD), f32)
        dk, dv = lax.fori_loop(j, NB, step, (zero, zero))
        dk = dk * (HD**-0.5)
        own[j, 0] = dk
        own[j, 1] = dv
        s1_src[j, 0] = dk.astype(bf16)
        s1_src[j, 1] = dv.astype(bf16)

    def s1(j):
        return remote(s1_src.at[j, 1 - core], s1_dst.at[j], s1_ss.at[j], s1_rs.at[j], c=sib)

    def s2(j):
        other = rows_of(1 - half, 256)
        return remote(
            s2_src.at[j, other], s2_dst.at[j], s2_ss.at[j], s2_rs.at[j], c=xh * 8 + (y + 1 - 2 * half) * 2 + core
        )

    def s1_done(j):
        s1(j).wait_recv()
        total = own[j, core] + s1_dst[j].astype(f32)
        s1_sum[j] = total
        s2_src[j] = total.astype(bf16)
        s2(j).start()

    def block_at(j, xh_, y_):
        rows = pl.ds(pl.multiple_of(j * B + (y_ % 2) * 256, 256), 256)
        cols = pl.ds(pl.multiple_of(core * 512 + (xh_ * 2 + y_ // 2) * HD, HD), HD)
        return rows, cols

    def s3(j, n, dx, dy):
        block = kv_all.at[block_at(j, xh, y)]
        return remote(block, block, s3_ss.at[j, n], s3_rs.at[j, xh * 4 + y], c=at(dx, dy, core))

    def s2_done(j):
        s2(j).wait_recv()
        total = s1_sum[j, rows_of(half, 256), :] + s2_dst[j].astype(f32)
        rows, cols = block_at(j, xh, y)
        kv_all[rows, cols] = total.astype(bf16)
        for n, (dx, dy) in enumerate(CHIPS):
            s3(j, n, dx, dy).start()

    def s4(j):
        part = kv_all.at[rows_of(j), pl.ds(pl.multiple_of(core * 512, 512), 512)]
        return remote(part, part, s4_ss.at[j], s4_rs.at[j], c=sib)

    def s3_done(j):
        for dx, dy in CHIPS:
            px, py = (xh + dx) % 2, (y + dy) % 4
            part = kv_all.at[block_at(j, px, py)]
            pltpu.make_async_copy(part, part, s3_rs.at[j, px * 4 + py]).wait()
        s4(j).start()

    def s4_done(j):
        part = kv_all.at[rows_of(j), pl.ds(pl.multiple_of((1 - core) * 512, 512), 512)]
        pltpu.make_async_copy(part, part, s4_rs.at[j]).wait()
        h = h_buf[:, :, j * B : (j + 1) * B].reshape(256, B)
        for n in range(4):
            cols = slice(n * 256, (n + 1) * 256)
            term = dot(h, kv_all[j * B : (j + 1) * B, cols])
            if j > 0:
                term = acc[:, cols] + term
            acc[:, cols] = term

    backward(0)
    s1(0).start()
    backward(1)
    s1(1).start()
    s1_done(0)
    backward(2)
    s1(2).start()
    s1_done(1)
    s2_done(0)
    backward(3)
    s1(3).start()
    s1_done(2)
    s2_done(1)
    s1_done(3)
    s2_done(2)
    s2_done(3)

    def h_wait(s, _):
        part = h_buf.at[:, :, rows_of(s, ROWS)]
        pltpu.make_async_copy(part, part, h_rs.at[s]).wait()
        return 0

    lax.fori_loop(0, 16, h_wait, 0)
    s3_done(0)
    s3_done(1)
    s4_done(0)
    s3_done(2)
    s4_done(1)
    s3_done(3)
    s4_done(2)
    s4_done(3)

    rs_src[...] = acc[...].astype(bf16).reshape(16, 16, 1024)

    def rs_copy(d):
        return remote(rs_src.at[d], rs_dst.at[dp], rs_ss.at[d], rs_rs.at[dp], d=d)

    def rs_send(n, _):
        rs_copy((dp + n) % 16).start()
        return 0

    lax.fori_loop(1, 16, rs_send, 0)
    grad_out[...] = acc[rows_of(dp, 16), :]

    def rs_add(n, _):
        d = (dp + 16 - n) % 16
        part = rs_dst.at[d]
        pltpu.make_async_copy(part, part, rs_rs.at[d]).wait()
        grad_out[...] += rs_dst[d].astype(f32)
        return 0

    lax.fori_loop(1, 16, rs_add, 0)

    def last(s, _):
        c = (me + s) % 16
        kv_part = kv_buf.at[0, my_rows]
        pltpu.make_async_copy(kv_part, kv_part, kv_ss.at[c]).wait()
        q_copy(c).wait_send()
        g_copy(c).wait_send()
        h_copy(c).wait_send()
        att_copy(c).wait_send()
        rs_copy((dp + s) % 16).wait_send()
        return 0

    lax.fori_loop(1, 16, last, 0)

    def att_wait(s, _):
        part = att_out.at[0, :, head_cols(s)]
        pltpu.make_async_copy(part, part, att_rs.at[s]).wait()
        return 0

    lax.fori_loop(0, 16, att_wait, 0)
    sib_copy.wait_send()
    for j in range(NB):
        s1(j).wait_send()
        s2(j).wait_send()
        for n, (dx, dy) in enumerate(CHIPS):
            s3(j, n, dx, dy).wait_send()
        s4(j).wait_send()


def per_device(hidden, queries, keys, values, upstream):
    sems = pltpu.SemaphoreType.DMA
    any_spec = pl.BlockSpec(memory_space=pl.ANY)
    pairs = NB * (NB + 1) // 2
    return pl.pallas_call(
        kernel,
        out_shape=(jax.ShapeDtypeStruct((1, ROWS, D), bf16), jax.ShapeDtypeStruct((16, 1024), f32)),
        in_specs=[any_spec] * 5,
        out_specs=(any_spec, pl.BlockSpec(memory_space=pltpu.VMEM)),
        scratch_shapes=[
            pltpu.VMEM((L, G2), bf16),
            pltpu.VMEM((L, G2), bf16),
            pltpu.VMEM((2, L, HD), bf16),
            pltpu.VMEM((ROWS, D), bf16),
            pltpu.VMEM((16, 16, 16, ROWS), bf16),
            pltpu.VMEM((16, 16, L), bf16),
            pltpu.VMEM((L, G2), bf16),
            pltpu.VMEM((NB, HD, B), bf16),
            pltpu.VMEM((HD, 2 * B), bf16),
            pltpu.VMEM((2, NB, B, 2 * B), f32),
            pltpu.VMEM((pairs, B, 2 * B), bf16),
            pltpu.VMEM((NB, HD, 2 * B), f32),
            pltpu.VMEM((NB, 8, 2 * B), f32),
            pltpu.VMEM((NB, HD, 2 * B), bf16),
            pltpu.VMEM((NB, 2 * B, HD), bf16),
            pltpu.VMEM((NB, 8, 2 * B), f32),
            pltpu.VMEM((NB, 2, B, HD), f32),
            pltpu.VMEM((NB, 2, B, HD), bf16),
            pltpu.VMEM((NB, B, HD), bf16),
            pltpu.VMEM((NB, B, HD), f32),
            pltpu.VMEM((NB, B, HD), bf16),
            pltpu.VMEM((NB, B // 2, HD), bf16),
            pltpu.VMEM((L, 1024), bf16),
            pltpu.VMEM((256, 1024), f32),
            pltpu.VMEM((16, 16, 1024), bf16),
            pltpu.VMEM((16, 16, 1024), bf16),
            sems((16,)), sems((16,)), sems((16,)), sems((16,)), sems((16,)), sems((16,)), sems, sems,
            sems((16,)), sems((16,)), sems((16,)), sems((16,)), sems,
            sems((NB,)), sems((NB,)), sems((NB,)), sems((NB,)), sems((NB, 7)), sems((NB, 8)),
            sems((NB,)), sems((NB,)), sems((16,)), sems((16,)),
        ],
        compiler_params=pltpu.CompilerParams(
            collective_id=0, has_side_effects=True, vmem_limit_bytes=56 * 2**20
        ),
        name="prefix_layer",
    )(hidden, queries, keys, values, upstream)


def solution(mesh):
    spec = P("dp", "ctx", None)
    return jax.shard_map(
        per_device,
        mesh=mesh,
        in_specs=(spec,) * 5,
        out_specs=(spec, P(("dp", "ctx"), None)),
        check_vma=False,
    )
```

time: 1610 us -> 120 us (0.07)
  waiting for transfers between devices: 1350 us -> 0 us
  Pallas kernels: 0 us -> 116 us
  matrix products: 95.1 us -> 0 us
  local copies, waits for them, and re-layouts: 60.9 us -> 2.95 us
  starting transfers between devices: 31.5 us -> 0 us
  blocking collectives: 21 us -> 0 us
  other arithmetic: 19.1 us -> 0 us
    unnamed x2 -> x0, waiting for transfers between devices: 1260 us -> none
    pallas_call x0 -> x1, Pallas kernels: none -> 116 us  [per_device(): pl.pallas_call(kernel, out_shape=(jax.ShapeDtypeStruct((1, ROWS, D), bf16...]
    dot_general x21 -> x0, matrix products: 95.1 us -> none  [the longest x4 31.4 us: block_step(): jnp.einsum('grqk,qgrd->kgrd', shares, grad_block, preferred_element_type=...]
    all_to_all x6 -> x0, waiting for transfers between devices: 86 us -> none  [the longest x1 17.1 us: per_device(): lax.all_to_all(value_terms, 'ctx', split_axis=0, concat_axis=1, tiled=True)]
    all_to_all x6 -> x0, starting transfers between devices: 31.5 us -> none  [the longest x1 8.45 us: per_device(): lax.all_to_all(value_send, 'ctx', split_axis=1, concat_axis=0, tiled=True)]
    unnamed x11 -> x4, local copies, waits for them, and re-layouts: 26.3 us -> 2.95 us
    all_to_all x1 -> x0, blocking collectives: 21 us -> none  [per_device(): lax.all_to_all(attended, 'ctx', split_axis=0, concat_axis=1, tiled=True)]
  transfers between devices with their start and end apart: 7 -> 0, of which waited for: 7 -> 0; matrix products, arithmetic and copies ran while one was open for 1% -> 0% of each run, Pallas kernels for 0% -> 0%
where the time goes in v1:
time: 120 us
  Pallas kernels  116 us (97%)
  local copies, waits for them, and re-layouts  2.95 us (2%)
    pallas_call x1, Pallas kernels, per_device(): pl.pallas_call(kernel, out_shape=(jax.ShapeDtypeStruct((1, ROWS, D), bf16...  116 us
    unnamed x4, local copies, waits for them, and re-layouts  2.95 us

profile of v1, /device:TPU:1, one launch (start us, length us, event | category | flops | bytes accessed | tf_op | source)
XLA Modules:
  0.0 119.7 jit_solution(2885928151738295424)
XLA Ops:
  0.6 116.1 %prefix_layer.1 = (bf16[1,128,4096]{2,1,0:T(8,128)(2,1)}, f32[16,1024]{1,0:T(8,128)}) custom-call(bf16[1,128,4096]{2,1,0:T(8,128)(2,1)} %hid_in.1, bf16[1,128,4096]{2,1,0:T(8,128)(2,1)} %q_in.1, bf16[1,128,512]{2,1,0:T(8,128)(2,1)} %k_in.1, bf16[1,128,512]{2,1,0:T(8,128)(2,1)} %v_in.1, bf16[1,128,4096]{2,1,0:T(8,128)(2,1)} %g_in.1), custom_call_target="tpu_custom_call" | custom-call | tf_op jit(solution)/shard_map/prefix_layer/pallas_call | solution.py:416
  116.7 0.0 copy-start
  116.7 2.3 %copy.9 = bf16[1,128,4096]{2,1,0:T(8,128)(2,1)} copy(bf16[1,128,4096]{2,1,0:T(8,128)(2,1)} %get-tuple-element.4) | data formatting | bytes 2097152
  119.0 0.0 copy-done
  119.0 0.6 copy.10
Async XLA Ops:
  116.7 2.3 %copy-start = (f32[16,1024]{1,0:T(8,128)S(1)}, f32[16,1024]{1,0:T(8,128)}, u32[]{:S(2)}) copy-start(f32[16,1024]{1,0:T(8,128)} %get-tuple-element.5) | copy-start | bytes 196612

commit v2 on v0

v2 whole, which is shorter than its diff:
```python
import math

import jax
import jax.numpy as jnp
from jax import lax
from jax.experimental import pallas as pl
from jax.experimental.pallas import tpu as pltpu
from jax.sharding import PartitionSpec as P

MESH = pl.DeviceIdType.MESH
HD = 128
L = 2048
ROWS = 128
BLK = 256
KB = 512
QC = 1024
D = 4096
EXP_SCALE = (HD**-0.5) * math.log2(math.e)
NEG = -1e30
f32 = jnp.float32
bf16 = jnp.bfloat16


def dot(a, b):
    return lax.dot_general(a, b, (((1,), (0,)), ((), ())), preferred_element_type=f32)


def col_max(s):
    return jnp.max(s.reshape(s.shape[0] // 8, 8, s.shape[1]), axis=0)


def col_sum(s):
    return jnp.sum(s.reshape(s.shape[0] // 8, 8, s.shape[1]), axis=0)


def part(i, n):
    return pl.ds(pl.multiple_of(i * n, n), n)


def kernel(
    hid_in, q_in, k_in, v_in, g_in, att_out, grad_out,
    q_buf, g_buf, kv_buf, hid_v, ht_src, h_buf, att_buf, vt, qt_scr, qs_scr, s_scr, p_scr, ot_scr, li_scr,
    gt_scr, gs_scr, dd_scr, own, y_src, y_dst, f_src, kv_all, acc, a_src, a_dst, rs_src, rs_dst,
    hid_sem, kv_ss, kv_rs, d_ss, d_rs, q_ss, q_rs, g_ss, g_rs, h_ss, h_rs, b_ss, b_rs, att_ss, att_rs,
    y_ss, y_rs, x_ss, x_rs, n_ss, n_rs, c_ss, c_rs, a_ss, a_rs, rs_ss, rs_rs,
):
    dp = lax.axis_index("dp")
    me = lax.axis_index("ctx")
    xh, y, core = me // 8, (me // 2) % 4, me % 2
    slot = xh * 2 + core
    sib = me + 1 - 2 * core
    partner = (me + 8) % 16

    def dev(x_, y_, c_):
        return x_ * 8 + y_ * 2 + c_

    def remote(src, dst, ss, rs, c=None, d=None):
        return pltpu.make_async_remote_copy(
            src_ref=src, dst_ref=dst, send_sem=ss, recv_sem=rs,
            device_id=(dp if d is None else d, me if c is None else c), device_id_type=MESH,
        )

    def local(src, dst, sem):
        return pltpu.make_async_copy(src, dst, sem)

    def arrived(ref, sem):
        pltpu.make_async_copy(ref, ref, sem).wait()

    quad = [dev(1 - xh, y, core), dev(1 - xh, y, 1 - core), sib]
    quad_slots = [(1 - xh) * 2 + core, (1 - xh) * 2 + 1 - core, xh * 2 + 1 - core]
    others = [(y + 1) % 4, (y + 3) % 4, (y + 2) % 4]
    z, xl = dp // 2, dp % 2
    x_quarters = [(1 - xh, xl), (xh, 1 - xl), (1 - xh, 1 - xl)]
    zs = [(z + n) % 8 for n in (4, 1, 7, 2, 6, 3, 5)]

    hid_copy = local(hid_in.at[0], hid_v, hid_sem)
    hid_copy.start()
    barrier = pltpu.get_barrier_semaphore()

    def greet(c=None, d=None):
        pl.semaphore_signal(
            barrier, inc=1, device_id=(dp if d is None else d, me if c is None else c), device_id_type=MESH
        )

    for c in quad[1:]:
        greet(c=c)
    for y_ in others:
        greet(c=dev(xh, y_, 0))
        greet(c=dev(xh, y_, 1))
    for x_, l_ in x_quarters:
        greet(c=dev(x_, y, core), d=z * 2 + l_)
    for z_ in zs:
        greet(d=z_ * 2 + xl)
    pl.semaphore_wait(barrier, 18)

    my_rows = part(me, ROWS)
    slot_rows = part(slot, ROWS)

    def kv_pair(s, which):
        return (k_in, v_in)[which].at[0, :, part(s, HD)], kv_buf.at[which, my_rows]

    def kv_copy(n, which):
        src, dst = kv_pair(quad_slots[n], which)
        return remote(src, dst, kv_ss.at[n, which], kv_rs.at[slot, which], c=quad[n])

    def needed(half, y_from, y_to):
        return (half == 0) | (y_to // 2 >= y_from // 2)

    def d_copy(n, c_, which):
        src, dst = kv_pair(xh * 2 + c_, which)
        return remote(src, dst, d_ss.at[n, c_, which], d_rs.at[y, core, which], c=dev(xh, others[n], c_))

    for n in range(3):
        for which in range(2):
            kv_copy(n, which).start()
    for which in range(2):
        src, dst = kv_pair(slot, which)
        local(src, dst, kv_rs.at[slot, which]).start()
    for n in range(3):

        @pl.when(needed(xh, y, others[n]))
        def _(n=n):
            for c_ in range(2):
                for which in range(2):
                    d_copy(n, c_, which).start()

    def q_copy(n):
        return remote(q_in.at[0, :, part(quad_slots[n], QC)], q_buf.at[slot_rows], q_ss.at[n], q_rs.at[slot], c=quad[n])

    def g_copy(n):
        return remote(g_in.at[0, :, part(quad_slots[n], QC)], g_buf.at[slot_rows], g_ss.at[n], g_rs.at[slot], c=quad[n])

    local(q_in.at[0, :, part(slot, QC)], q_buf.at[slot_rows], q_rs.at[slot]).start()
    local(g_in.at[0, :, part(slot, QC)], g_buf.at[slot_rows], g_rs.at[slot]).start()
    q_copy(2).start()

    hid_copy.wait()

    def turn(b, _):
        ht_src[b] = hid_v[:, part(b, 256)].T.reshape(2, 8, 16, ROWS)
        return 0

    lax.fori_loop(0, 16, turn, 0)

    for n in range(2):
        q_copy(n).start()

    def kv_wait(x_):
        for c_ in range(2):
            for which in range(2):
                arrived(kv_buf.at[which, part(dev(x_, y, c_), ROWS)], kv_rs.at[x_ * 2 + c_, which])

    def b_copy(n):
        rows = kv_buf.at[:, part((1 - xh) * 4 + y, BLK)]
        return remote(rows, rows, b_ss.at[n], b_rs.at[y], c=dev(xh, others[n], core))

    kv_wait(1 - xh)
    for n in range(3):

        @pl.when(needed(1 - xh, y, others[n]))
        def _(n=n):
            b_copy(n).start()

    kv_wait(xh)

    row_devices = [(y_, c_) for y_ in others for c_ in (core, 1 - core)] + [(y, 1 - core)]

    def h_dst():
        return h_buf.at[:, :, :, part(y * 2 + core, ROWS)]

    def h_copy(n):
        y_, c_ = row_devices[n]
        return remote(
            ht_src.at[:, :, y_ * 2 + c_], h_dst(), h_ss.at[n], h_rs.at[y * 2 + core], c=dev(xh, y_, c_)
        )

    local(ht_src.at[:, :, y * 2 + core], h_dst(), h_rs.at[y * 2 + core]).start()

    def turn_v(j):
        vt[j] = kv_buf[1, j * KB : (j + 1) * KB, :].T

    def b_wait(half):
        for y_ in others:
            wanted = needed(half, y_, y)

            @pl.when(wanted & (xh == half))
            def _(y_=y_):
                for c_ in range(2):
                    for which in range(2):
                        arrived(kv_buf.at[which, part(dev(xh, y_, c_), ROWS)], d_rs.at[y_, c_, which])

            @pl.when(wanted & (xh != half))
            def _(y_=y_):
                arrived(kv_buf.at[:, part(half * 4 + y_, BLK)], b_rs.at[y_])

        turn_v(2 * half)
        turn_v(2 * half + 1)

    halves = [xh, xh, 1 - xh, 1 - xh]
    counts = [y // 2 + 1 + 2 * h for h in halves]

    def wait_slots(buf, sems, half):
        for c_ in range(2):
            s = half * 2 + c_
            arrived(buf.at[part(s, ROWS)], sems.at[s])

    def turn_q(u):
        rows = part(halves[u], BLK)
        heads = [q_buf[rows, (u % 2) * KB + h * HD : (u % 2) * KB + (h + 1) * HD] for h in range(4)]
        qt_scr[...] = jnp.concatenate([h.T for h in heads], axis=1)
        qs_scr[halves[u] * 2 + u % 2] = jnp.concatenate(heads, axis=0)

    def k_block(j):
        return kv_buf[0, part(j, KB), :]

    def scores(u, j, mn):
        s = dot(k_block(j), qt_scr[...])
        s_scr[u % 2, j] = s
        return jnp.maximum(mn, col_max(s))

    def last_scores(u, mn):
        s = dot(k_block(counts[u] - 1), qt_scr[...])
        key_at = lax.broadcasted_iota(jnp.int32, (KB, QC), 0)
        query_at = lax.broadcasted_iota(jnp.int32, (KB, QC), 1) % BLK + (y % 2) * BLK
        s = jnp.where(key_at <= query_at, s, NEG)
        s_scr[u % 2, counts[u] - 1] = s
        return jnp.maximum(mn, col_max(s))

    def p_at(t, j):
        return jnp.where(t < 2, t * 2, t * 4 - 4) + j

    no_max = jnp.full((8, QC), NEG, f32)

    def att_copy(u, c_):
        s = halves[u] * 2 + c_
        cols = pl.ds(pl.multiple_of(slot * QC + (u % 2) * KB, KB), KB)
        src = att_buf.at[part(s, ROWS), (u % 2) * KB : (u % 2 + 1) * KB]
        return s, src, att_out.at[0, :, cols], att_rs.at[slot, u % 2]

    def att_remote(u, c_):
        s, src, dst, sem = att_copy(u, c_)
        return remote(src, dst, att_ss.at[u, c_], sem, c=dev(halves[u], y, c_))

    def forward(u, top):
        half, n = halves[u], counts[u]
        t = half * 2 + u % 2
        shift = jnp.max(top, axis=0, keepdims=True) * EXP_SCALE
        if u == 1:
            wait_slots(q_buf, q_rs, 1 - xh)

            @pl.when(xh == 0)
            def _():
                b_wait(1)

        if u < 3:
            turn_q(u + 1)

        def weigh(j, carry):
            l, o, mn = carry
            e = jnp.exp2(s_scr[u % 2, j] * EXP_SCALE - shift)
            l = l + col_sum(e)
            eb = e.astype(bf16)
            p_scr[p_at(t, j)] = eb
            return l, o + dot(vt[j], eb), mn

        def both(j, carry):
            l, o, mn = carry
            return weigh(j, (l, o, scores(u + 1, j, mn)))

        carry = (jnp.zeros((8, QC), f32), jnp.zeros((HD, QC), f32), no_max)
        if u == 3:
            l, o, mn = lax.fori_loop(0, n, weigh, carry)
        elif u == 1:
            m = counts[2] - 1
            shared = jnp.minimum(n, m)
            carry = lax.fori_loop(0, shared, both, carry)
            l, o, mn = lax.fori_loop(shared, n, weigh, carry)
            mn = lax.fori_loop(shared, m, lambda j, mx: scores(2, j, mx), mn)
            mn = last_scores(2, mn)
        else:
            carry = lax.fori_loop(0, n - 1, both, carry)
            l, o, mn = weigh(n - 1, carry)
            mn = last_scores(u + 1, mn)
        li = 1.0 / jnp.sum(l, axis=0, keepdims=True)
        o = o * li
        ot_scr[t] = o
        li_scr[t] = jnp.broadcast_to(li, (8, QC))
        rows = part(half, BLK)
        for h in range(4):
            cols = slice((u % 2) * KB + h * HD, (u % 2) * KB + (h + 1) * HD)
            att_buf[rows, cols] = o[:, h * BLK : (h + 1) * BLK].T.astype(bf16)
        for c_ in range(2):
            s, src, dst, sem = att_copy(u, c_)

            @pl.when(s == slot)
            def _(src=src, dst=dst, sem=sem):
                local(src, dst, sem).start()

            @pl.when(s != slot)
            def _(c_=c_):
                att_remote(u, c_).start()

        return mn

    wait_slots(q_buf, q_rs, xh)
    turn_q(0)
    b_wait(0)
    for n in (2, 0, 1):
        g_copy(n).start()
    for n in range(7):
        h_copy(n).start()
    early = jnp.minimum(counts[0] - 1, 2)
    top = lax.fori_loop(0, early, lambda j, mx: scores(0, j, mx), no_max)

    @pl.when(xh == 1)
    def _():
        b_wait(1)

    top = lax.fori_loop(early, counts[0] - 1, lambda j, mx: scores(0, j, mx), top)
    top = last_scores(0, top)
    for u in range(4):
        top = forward(u, top)

    for half in range(2):
        wait_slots(g_buf, g_rs, half)

    def prepare(t, _):
        rows = part(t // 2, BLK)
        heads = [g_buf[rows, pl.ds(pl.multiple_of((t % 2) * KB + h * HD, HD), HD)].T for h in range(4)]
        gt = jnp.concatenate(heads, axis=1).astype(f32)
        gs = (gt * li_scr[t][0:1, :]).astype(bf16)
        gt_scr[t] = gs
        gs_scr[t] = gs.T
        dd = jnp.sum(gs.astype(f32) * ot_scr[t], axis=0, keepdims=True)
        dd_scr[t] = jnp.broadcast_to(dd, (8, QC))
        return 0

    lax.fori_loop(0, 4, prepare, 0)

    def y_copy(half, y_to):
        return remote(
            y_src.at[half * 4 + y_to], y_dst.at[half, y], y_ss.at[half * 4 + y_to], y_rs.at[half, y],
            c=dev(xh, y_to, core),
        )

    def y_needed(half, y_from, y_to):
        return (y_from != y_to) if half == 0 else (y_from > y_to)

    def backward(j):
        vj = kv_buf[1, j * KB : (j + 1) * KB, :]
        first = (0, jnp.where(y >= 2, 0, 2), 2, jnp.where(y >= 2, 2, 4))[j]

        def step(t, carry):
            dk, dv = carry
            eb = p_scr[p_at(t, j)]
            dpr = dot(vj, gt_scr[t])
            ds = (eb.astype(f32) * (dpr - dd_scr[t][0:1, :])).astype(bf16)
            return dk + dot(ds, qs_scr[t]), dv + dot(eb, gs_scr[t])

        zero = jnp.zeros((KB, HD), f32)
        dk, dv = lax.fori_loop(first, 4, step, (zero, zero))
        dk = dk * (HD**-0.5)
        half = j // 2
        for b in range(2):
            y_to = (2 * j + b) % 4
            for which, grad in enumerate((dk, dv)):
                piece = grad[b * BLK : (b + 1) * BLK]
                own[half * 4 + y_to, which] = piece
                y_src[half * 4 + y_to, which] = piece.astype(bf16)

            @pl.when(y_needed(half, y, y_to))
            def _(half=half, y_to=y_to):
                y_copy(half, y_to).start()

    def block(p, y_, c_):
        return kv_all.at[pl.ds(c_ * 4 + p * 2, 2), part(y_, BLK)]

    def x_copy():
        return remote(f_src, block(xh, y, core), x_ss, x_rs, c=partner)

    def n_copy(p, n):
        return remote(block(p, y, core), block(p, y, core), n_ss.at[p, n], n_rs.at[p, y], c=dev(xh, others[n], core))

    def c_copy(p, y_):
        return remote(block(p, y_, core), block(p, y_, core), c_ss.at[p, y_], c_rs.at[p, y_], c=sib)

    def spread(p):
        for n in range(3):
            n_copy(p, n).start()
        c_copy(p, y).start()

    def y_sum(half):
        at = half * 4 + y
        for n in range(3):

            @pl.when(y_needed(half, others[n], y))
            def _(n=n):
                arrived(y_dst.at[half, others[n]], y_rs.at[half, others[n]])
                own[at] = own[at] + y_dst[half, others[n]].astype(f32)

        @pl.when(xh == half)
        def _():
            kv_all[pl.ds(core * 4 + xh * 2, 2), part(y, BLK)] = own[at].astype(bf16)
            spread(xh)

        @pl.when(xh != half)
        def _():
            f_src[...] = own[at].astype(bf16)
            x_copy().start()

    backward(2)
    backward(3)
    backward(0)
    y_sum(1)

    @pl.when(y < 2)
    def _():
        y_sum(0)

    backward(1)

    @pl.when(y >= 2)
    def _():
        y_sum(0)

    arrived(block(1 - xh, y, core), x_rs)
    spread(1 - xh)
    for s in range(8):
        arrived(h_buf.at[:, :, :, part(s, ROWS)], h_rs.at[s])

    def project(y_):
        for p in range(2):
            arrived(block(p, y_, 1 - core), c_rs.at[p, y_])
        h = h_buf[:, :, :, y_ * BLK : (y_ + 1) * BLK].reshape(512, BLK)
        rows = slice(y_ * BLK, (y_ + 1) * BLK)
        for n in range(4):
            kv = jnp.concatenate([kv_all[2 * n, rows, :], kv_all[2 * n + 1, rows, :]], axis=1)
            term = dot(h, kv).reshape(8, 2, 2, 16, 256)
            cols = slice(n * 256, (n + 1) * 256)
            if y_ > 0:
                term = acc[:, :, :, :, cols] + term
            acc[:, :, :, :, cols] = term

    for y_ in range(4):

        @pl.when(y != y_)
        def _(y_=y_):
            for p in range(2):
                arrived(block(p, y_, core), n_rs.at[p, y_])
                c_copy(p, y_).start()

        if y_ > 0:
            project(y_ - 1)
    project(3)

    def out_cols(b):
        c_, x_, which = b // 4, (b // 2) % 2, b % 2
        at = which * 512 + (x_ * 2 + c_) * HD
        return slice(at, at + HD)

    def a_copy(n, z_):
        x_, l_ = x_quarters[n]
        return remote(
            a_src.at[n, z_], a_dst.at[n, z_], a_ss.at[n, z_], a_rs.at[n, z_], c=dev(x_, y, core), d=z * 2 + l_
        )

    def rs_copy(z_):
        return remote(rs_src.at[z_], rs_dst.at[z], rs_ss.at[z_], rs_rs.at[z], d=z_ * 2 + xl)

    for z_ in [*zs, z]:
        for n, (x_, l_) in enumerate(x_quarters):
            for b in range(8):
                a_src[n, z_, :, out_cols(b)] = acc[z_, l_, x_, :, b * HD : (b + 1) * HD].astype(bf16)
            a_copy(n, z_).start()

    def x_total(z_, b):
        total = acc[z_, xl, xh, :, b * HD : (b + 1) * HD]
        for n in range(3):
            total = total + a_dst[n, z_, :, out_cols(b)].astype(f32)
        return total

    for z_ in zs:
        for n in range(3):
            arrived(a_dst.at[n, z_], a_rs.at[n, z_])
        for b in range(8):
            rs_src[z_, :, out_cols(b)] = x_total(z_, b).astype(bf16)
        rs_copy(z_).start()
    for n in range(3):
        arrived(a_dst.at[n, z], a_rs.at[n, z])
    for b in range(8):
        grad_out[:, out_cols(b)] = x_total(z, b)
    for z_ in zs:
        arrived(rs_dst.at[z_], rs_rs.at[z_])
        grad_out[...] += rs_dst[z_].astype(f32)

    for n in range(3):
        for which in range(2):
            kv_copy(n, which).wait_send()
        q_copy(n).wait_send()
        g_copy(n).wait_send()
        for p in range(2):
            n_copy(p, n).wait_send()

        @pl.when(needed(xh, y, others[n]))
        def _(n=n):
            for c_ in range(2):
                for which in range(2):
                    d_copy(n, c_, which).wait_send()

        @pl.when(needed(1 - xh, y, others[n]))
        def _(n=n):
            b_copy(n).wait_send()

    for n in range(7):
        h_copy(n).wait_send()
    for u in range(4):
        for c_ in range(2):

            @pl.when(halves[u] * 2 + c_ != slot)
            def _(u=u, c_=c_):
                att_remote(u, c_).wait_send()

    for s in range(4):
        for hh in range(2):
            cols = pl.ds(pl.multiple_of(s * QC + hh * KB, KB), KB)
            arrived(att_out.at[0, :, cols], att_rs.at[s, hh])
    for half in range(2):
        for y_ in range(4):

            @pl.when(y_needed(half, y, y_))
            def _(half=half, y_=y_):
                y_copy(half, y_).wait_send()

    x_copy().wait_send()
    for y_ in range(4):
        for p in range(2):
            c_copy(p, y_).wait_send()
    for z_ in range(8):
        for n in range(3):
            a_copy(n, z_).wait_send()
    for z_ in zs:
        rs_copy(z_).wait_send()


def per_device(hidden, queries, keys, values, upstream):
    sems = pltpu.SemaphoreType.DMA
    any_spec = pl.BlockSpec(memory_space=pl.ANY)
    return pl.pallas_call(
        kernel,
        out_shape=(jax.ShapeDtypeStruct((1, ROWS, D), bf16), jax.ShapeDtypeStruct((16, 1024), f32)),
        in_specs=[any_spec] * 5,
        out_specs=(any_spec, pl.BlockSpec(memory_space=pltpu.VMEM)),
        scratch_shapes=[
            pltpu.VMEM((4 * ROWS, QC), bf16),
            pltpu.VMEM((4 * ROWS, QC), bf16),
            pltpu.VMEM((2, L, HD), bf16),
            pltpu.VMEM((ROWS, D), bf16),
            pltpu.VMEM((16, 2, 8, 16, ROWS), bf16),
            pltpu.VMEM((16, 2, 16, L // 2), bf16),
            pltpu.VMEM((4 * ROWS, QC), bf16),
            pltpu.VMEM((4, HD, KB), bf16),
            pltpu.VMEM((HD, QC), bf16),
            pltpu.VMEM((4, QC, HD), bf16),
            pltpu.VMEM((2, 4, KB, QC), f32),
            pltpu.VMEM((12, KB, QC), bf16),
            pltpu.VMEM((4, HD, QC), f32),
            pltpu.VMEM((4, 8, QC), f32),
            pltpu.VMEM((4, HD, QC), bf16),
            pltpu.VMEM((4, QC, HD), bf16),
            pltpu.VMEM((4, 8, QC), f32),
            pltpu.VMEM((8, 2, BLK, HD), f32),
            pltpu.VMEM((8, 2, BLK, HD), bf16),
            pltpu.VMEM((2, 4, 2, BLK, HD), bf16),
            pltpu.VMEM((2, BLK, HD), bf16),
            pltpu.VMEM((8, L // 2, HD), bf16),
            pltpu.VMEM((8, 2, 2, 16, 1024), f32),
            pltpu.VMEM((3, 8, 16, 1024), bf16),
            pltpu.VMEM((3, 8, 16, 1024), bf16),
            pltpu.VMEM((8, 16, 1024), bf16),
            pltpu.VMEM((8, 16, 1024), bf16),
            sems, sems((3, 2)), sems((4, 2)), sems((3, 2, 2)), sems((4, 2, 2)), sems((3,)), sems((4,)), sems((3,)), sems((4,)),
            sems((7,)), sems((8,)), sems((3,)), sems((4,)), sems((4, 2)), sems((4, 2)),
            sems((8,)), sems((2, 4)), sems, sems, sems((2, 3)), sems((2, 4)), sems((2, 4)), sems((2, 4)),
            sems((3, 8)), sems((3, 8)), sems((8,)), sems((8,)),
        ],
        compiler_params=pltpu.CompilerParams(
            collective_id=0, has_side_effects=True, vmem_limit_bytes=61 * 2**20
        ),
        name="prefix_layer",
    )(hidden, queries, keys, values, upstream)


def solution(mesh):
    spec = P("dp", "ctx", None)
    return jax.shard_map(
        per_device,
        mesh=mesh,
        in_specs=(spec,) * 5,
        out_specs=(spec, P(("dp", "ctx"), None)),
        check_vma=False,
    )
```

time: 1610 us -> 109 us (0.07)
  waiting for transfers between devices: 1350 us -> 0 us
  Pallas kernels: 0 us -> 104 us
  matrix products: 95.1 us -> 0 us
  local copies, waits for them, and re-layouts: 60.9 us -> 2.95 us
  starting transfers between devices: 31.5 us -> 0 us
  blocking collectives: 21 us -> 0 us
  other arithmetic: 19.1 us -> 0 us
    unnamed x2 -> x0, waiting for transfers between devices: 1260 us -> none
    pallas_call x0 -> x1, Pallas kernels: none -> 104 us  [per_device(): pl.pallas_call(kernel, out_shape=(jax.ShapeDtypeStruct((1, ROWS, D), bf16...]
    dot_general x21 -> x0, matrix products: 95.1 us -> none  [the longest x4 31.4 us: block_step(): jnp.einsum('grqk,qgrd->kgrd', shares, grad_block, preferred_element_type=...]
    all_to_all x6 -> x0, waiting for transfers between devices: 86 us -> none  [the longest x1 17.1 us: per_device(): lax.all_to_all(value_terms, 'ctx', split_axis=0, concat_axis=1, tiled=True)]
    all_to_all x6 -> x0, starting transfers between devices: 31.5 us -> none  [the longest x1 8.45 us: per_device(): lax.all_to_all(value_send, 'ctx', split_axis=1, concat_axis=0, tiled=True)]
    unnamed x11 -> x4, local copies, waits for them, and re-layouts: 26.3 us -> 2.95 us
    all_to_all x1 -> x0, blocking collectives: 21 us -> none  [per_device(): lax.all_to_all(attended, 'ctx', split_axis=0, concat_axis=1, tiled=True)]
  transfers between devices with their start and end apart: 7 -> 0, of which waited for: 7 -> 0; matrix products, arithmetic and copies ran while one was open for 1% -> 0% of each run, Pallas kernels for 0% -> 0%
where the time goes in v2:
time: 109 us; the launch traced here: 108 us
  Pallas kernels  104 us (95%)
  local copies, waits for them, and re-layouts  2.95 us (3%)
    pallas_call x1, Pallas kernels, per_device(): pl.pallas_call(kernel, out_shape=(jax.ShapeDtypeStruct((1, ROWS, D), bf16...  104 us
    unnamed x4, local copies, waits for them, and re-layouts  2.95 us

profile of v2, /device:TPU:1, one launch (start us, length us, event | category | flops | bytes accessed | tf_op | source)
XLA Modules:
  0.0 108.0 jit_solution(9283515203996571592)
XLA Ops:
  0.6 104.4 %prefix_layer.1 = (bf16[1,128,4096]{2,1,0:T(8,128)(2,1)}, f32[16,1024]{1,0:T(8,128)}) custom-call(bf16[1,128,4096]{2,1,0:T(8,128)(2,1)} %hid_in.1, bf16[1,128,4096]{2,1,0:T(8,128)(2,1)} %q_in.1, bf16[1,128,512]{2,1,0:T(8,128)(2,1)} %k_in.1, bf16[1,128,512]{2,1,0:T(8,128)(2,1)} %v_in.1, bf16[1,128,4096]{2,1,0:T(8,128)(2,1)} %g_in.1), custom_call_target="tpu_custom_call" | custom-call | tf_op jit(solution)/shard_map/prefix_layer/pallas_call | solution.py:548
  105.0 0.0 copy-start
  105.0 2.3 %copy.9 = bf16[1,128,4096]{2,1,0:T(8,128)(2,1)} copy(bf16[1,128,4096]{2,1,0:T(8,128)(2,1)} %get-tuple-element.4) | data formatting | bytes 2097152
  107.3 0.0 copy-done
  107.3 0.6 copy.10
Async XLA Ops:
  105.0 2.3 %copy-start = (f32[16,1024]{1,0:T(8,128)S(1)}, f32[16,1024]{1,0:T(8,128)}, u32[]{:S(2)}) copy-start(f32[16,1024]{1,0:T(8,128)} %get-tuple-element.5) | copy-start | bytes 196612

commit v3 on v2

--- a/solution.py
+++ b/solution.py
@@ -408,23 +408,18 @@
             f_src[...] = own[at].astype(bf16)
             x_copy().start()
 
+    def relay():
+        arrived(block(1 - xh, y, core), x_rs)
+        spread(1 - xh)
+
+    backward(0)
+    backward(1)
     backward(2)
     backward(3)
-    backward(0)
+    y_sum(0)
     y_sum(1)
-
-    @pl.when(y < 2)
-    def _():
-        y_sum(0)
-
-    backward(1)
-
-    @pl.when(y >= 2)
-    def _():
-        y_sum(0)
-
-    arrived(block(1 - xh, y, core), x_rs)
-    spread(1 - xh)
+    relay()
+
     for s in range(8):
         arrived(h_buf.at[:, :, :, part(s, ROWS)], h_rs.at[s])
 

time: 109 us -> 96.3 us (0.88)
  Pallas kernels: 104 us -> 92.1 us
    pallas_call x1, Pallas kernels: 104 us -> 92.1 us  [per_device(): pl.pallas_call(kernel, out_shape=(jax.ShapeDtypeStruct((1, ROWS, D), bf16...]
where the time goes in v3:
time: 96.3 us; the launch traced here: 95.7 us
  Pallas kernels  92.1 us (96%)
  local copies, waits for them, and re-layouts  2.95 us (3%)
    pallas_call x1, Pallas kernels, per_device(): pl.pallas_call(kernel, out_shape=(jax.ShapeDtypeStruct((1, ROWS, D), bf16...  92.1 us
    unnamed x4, local copies, waits for them, and re-layouts  2.95 us

profile of v3, /device:TPU:1, one launch (start us, length us, event | category | flops | bytes accessed | tf_op | source)
XLA Modules:
  0.0 95.7 jit_solution(6419790836117602579)
XLA Ops:
  0.6 92.1 %prefix_layer.1 = (bf16[1,128,4096]{2,1,0:T(8,128)(2,1)}, f32[16,1024]{1,0:T(8,128)}) custom-call(bf16[1,128,4096]{2,1,0:T(8,128)(2,1)} %hid_in.1, bf16[1,128,4096]{2,1,0:T(8,128)(2,1)} %q_in.1, bf16[1,128,512]{2,1,0:T(8,128)(2,1)} %k_in.1, bf16[1,128,512]{2,1,0:T(8,128)(2,1)} %v_in.1, bf16[1,128,4096]{2,1,0:T(8,128)(2,1)} %g_in.1), custom_call_target="tpu_custom_call" | custom-call | tf_op jit(solution)/shard_map/prefix_layer/pallas_call | solution.py:543
  92.7 0.0 copy-start
  92.7 2.3 %copy.9 = bf16[1,128,4096]{2,1,0:T(8,128)(2,1)} copy(bf16[1,128,4096]{2,1,0:T(8,128)(2,1)} %get-tuple-element.4) | data formatting | bytes 2097152
  95.1 0.0 copy-done
  95.1 0.6 copy.10
Async XLA Ops:
  92.7 2.3 %copy-start = (f32[16,1024]{1,0:T(8,128)S(1)}, f32[16,1024]{1,0:T(8,128)}, u32[]{:S(2)}) copy-start(f32[16,1024]{1,0:T(8,128)} %get-tuple-element.5) | copy-start | bytes 196612

commit v4 on v3

--- a/solution.py
+++ b/solution.py
@@ -144,6 +144,8 @@
 
     for n in range(2):
         q_copy(n).start()
+    for n in (2, 0, 1):
+        g_copy(n).start()
 
     def kv_wait(x_):
         for c_ in range(2):
@@ -305,8 +307,6 @@
     wait_slots(q_buf, q_rs, xh)
     turn_q(0)
     b_wait(0)
-    for n in (2, 0, 1):
-        g_copy(n).start()
     for n in range(7):
         h_copy(n).start()
     early = jnp.minimum(counts[0] - 1, 2)

time: 96.3 us -> 96 us (level)
  no operation moved by 1% of the time
where the time goes in v4:
time: 96 us; the launch traced here: 95.9 us
  Pallas kernels  92.3 us (96%)
  local copies, waits for them, and re-layouts  2.95 us (3%)
    pallas_call x1, Pallas kernels, per_device(): pl.pallas_call(kernel, out_shape=(jax.ShapeDtypeStruct((1, ROWS, D), bf16...  92.3 us
    unnamed x4, local copies, waits for them, and re-layouts  2.95 us

profile of v4, /device:TPU:1, one launch (start us, length us, event | category | flops | bytes accessed | tf_op | source)
XLA Modules:
  0.0 95.9 jit_solution(11754417029519135990)
XLA Ops:
  0.6 92.3 %prefix_layer.1 = (bf16[1,128,4096]{2,1,0:T(8,128)(2,1)}, f32[16,1024]{1,0:T(8,128)}) custom-call(bf16[1,128,4096]{2,1,0:T(8,128)(2,1)} %hid_in.1, bf16[1,128,4096]{2,1,0:T(8,128)(2,1)} %q_in.1, bf16[1,128,512]{2,1,0:T(8,128)(2,1)} %k_in.1, bf16[1,128,512]{2,1,0:T(8,128)(2,1)} %v_in.1, bf16[1,128,4096]{2,1,0:T(8,128)(2,1)} %g_in.1), custom_call_target="tpu_custom_call" | custom-call | tf_op jit(solution)/shard_map/prefix_layer/pallas_call | solution.py:543
  92.9 0.0 copy-start
  92.9 2.3 %copy.9 = bf16[1,128,4096]{2,1,0:T(8,128)(2,1)} copy(bf16[1,128,4096]{2,1,0:T(8,128)(2,1)} %get-tuple-element.4) | data formatting | bytes 2097152
  95.2 0.0 copy-done
  95.2 0.6 copy.10
Async XLA Ops:
  92.9 2.3 %copy-start = (f32[16,1024]{1,0:T(8,128)S(1)}, f32[16,1024]{1,0:T(8,128)}, u32[]{:S(2)}) copy-start(f32[16,1024]{1,0:T(8,128)} %get-tuple-element.5) | copy-start | bytes 196612
